TPU v7x, 32 devices: a whole 2x2x4 slice. The times are simulated.
32 devices in a mesh: dp: 4 (over z), sq: 8 (over y, x, core).
Axes of the slice: x: 2, y: 2, z: 4, core: 2. Of those that a mesh axis runs over, the one named last changes fastest.
Arguments:
- frames: bfloat16 [4, 1024, 1024], P('dp', 'sq'), may hold values from -6 to 6
- norm1_gain: float32 [1024], replicated, may hold values from 0.5 to 1.5
- w_qkv: bfloat16 [1024, 3072], replicated, may hold values from -0.1875 to 0.1875
- w_out: bfloat16 [1024, 1024], replicated, may hold values from -0.75 to 0.75
- norm2_gain: float32 [1024], replicated, may hold values from 0.5 to 1.5
- w_up: bfloat16 [1024, 4096], replicated, may hold values from -0.1875 to 0.1875
- w_down: bfloat16 [4096, 1024], replicated, may hold values from -0.09375 to 0.09375
- lengths: int32 [4, 8], P('dp'), may hold values from 1 to 896, as said below
- cotangent: bfloat16 [4, 1024, 1024], P('dp', 'sq'), may hold values from -6 to 6
Outputs:
- out: bfloat16 [4, 1024, 1024], P('dp', 'sq')
- d_in: float32 [4, 1024, 1024], P('dp', 'sq')
- g_norm1: float32 [1024], P('sq')
- g_qkv: float32 [1024, 3072], P('sq')
- g_out: float32 [1024, 1024], P('sq')
- g_norm2: float32 [1024], P('sq')
- g_up: float32 [1024, 4096], P('sq')
- g_down: float32 [4096, 1024], P('sq')
Inputs may be any that keep to these rules, and one draw needn't show every extreme that they name: Each row's lengths sum to 1024. In each row exactly one item has 896 frames and is neither the first nor the last item of the row; the other items share the remaining 128 frames.
All inputs are finite; a program needn't handle non-finite values.
Results may differ from a plain program's by a relative error of at most 0.025.
Values may be sent and summed in bfloat16 or wider, within the bound.
A program may use at most 256 MiB of HBM per device.

v0:
```python
import jax
import jax.numpy as jnp
from jax import lax
from jax.sharding import PartitionSpec as P

HEADS = 16
HEAD_DIM = 64
EPSILON = 1e-05
NEG_FILL = -1000000000.0
START_MAX = -1e30


def norm_scaled(values, gain):
    return values * lax.rsqrt(jnp.mean(values * values, axis=-1, keepdims=True) + EPSILON) * gain


def segment_ids(positions, item_ends):
    return jnp.sum((positions[None, :, None] >= item_ends[:, None, :]).astype(jnp.int32), axis=2)


def visible(query_pos, query_seg, key_pos, key_seg):
    return (key_pos[None, None, :] <= query_pos[None, :, None]) & (
        key_seg[:, None, :] == query_seg[:, :, None]
    )


def block_size(count, limit):
    for candidate in range(min(count, limit), 0, -1):
        if count % candidate == 0:
            return candidate
    return count


def over_blocks(carry, arrays, start, step_fn, limit):
    count = arrays[0].shape[1]
    size = block_size(count, limit)
    number = count // size
    if number == 1:
        return step_fn(carry, arrays, start)
    stacked = tuple(
        (
            jnp.swapaxes(member.reshape((member.shape[0], number, size) + member.shape[2:]), 0, 1)
            for member in arrays
        )
    )

    def turn(state, item):
        offset, pieces = item
        return (step_fn(state, pieces, start + offset * size), None)

    offsets = jnp.arange(number, dtype=jnp.int32)
    return lax.scan(turn, carry, (offsets, stacked))[0]


def contract_rows(left, right):
    return lax.dot_general(
        left, right, (((0,), (0,)), ((), ())), preferred_element_type=jnp.float32
    )


def times_transpose(left, right):
    return lax.dot_general(
        left, right, (((1,), (1,)), ((), ())), preferred_element_type=jnp.float32
    )


def heads_flat(values, batch, rows, width):
    return values.transpose(0, 2, 1, 3).reshape(batch * rows, width)


def shards(frames, norm1_gain, w_qkv, w_out, norm2_gain, w_up, w_down, lengths, cotangent):
    batch = frames.shape[0]
    rows = frames.shape[1]
    width = frames.shape[2]
    factor = HEAD_DIM ** (-0.5)
    first = lax.axis_index("sq") * rows
    query_pos = first + jnp.arange(rows, dtype=jnp.int32)
    item_ends = jnp.cumsum(lengths, axis=1)
    query_seg = segment_ids(query_pos, item_ends)
    frames_own = frames.reshape(batch * rows, width).astype(jnp.float32)
    hidden1, norm1_pull = jax.vjp(norm_scaled, frames_own, norm1_gain)
    hidden1_low = hidden1.astype(jnp.bfloat16)
    mixed = jnp.dot(hidden1_low, w_qkv, preferred_element_type=jnp.float32).astype(jnp.bfloat16)
    query_rows = mixed[:, :width].reshape(batch, rows, width)
    key_rows = mixed[:, width : 2 * width].reshape(batch, rows, width)
    value_rows = mixed[:, 2 * width :].reshape(batch, rows, width)
    queries = query_rows.reshape(batch, rows, HEADS, HEAD_DIM)
    keys_own = key_rows.reshape(batch, rows, HEADS, HEAD_DIM)
    values_own = value_rows.reshape(batch, rows, HEADS, HEAD_DIM)

    def forward_step(carry, pieces, start):
        key_piece, value_piece = pieces
        count = key_piece.shape[1]
        key_pos = start + jnp.arange(count, dtype=jnp.int32)
        key_seg = segment_ids(key_pos, item_ends)

        def forward_work(state):
            running_max, running_sum, accum = state
            keys_block = key_piece.reshape(batch, count, HEADS, HEAD_DIM)
            values_block = value_piece.reshape(batch, count, HEADS, HEAD_DIM)
            scores = (
                jnp.einsum(
                    "rqhd,rkhd->rhqk", queries, keys_block, preferred_element_type=jnp.float32
                )
                * factor
            )
            mask = visible(query_pos, query_seg, key_pos, key_seg)[:, None]
            scores = jnp.where(mask, scores, NEG_FILL)
            new_max = jnp.maximum(running_max, jnp.max(scores, axis=-1))
            weights = jnp.where(mask, jnp.exp(scores - new_max[..., None]), 0.0)
            decay = jnp.exp(running_max - new_max)
            new_sum = decay * running_sum + jnp.sum(weights, axis=-1)
            update = jnp.einsum(
                "rhqk,rkhd->rhqd",
                weights.astype(jnp.bfloat16),
                values_block,
                preferred_element_type=jnp.float32,
            )
            return (new_max, new_sum, decay[..., None] * accum + update)

        return lax.cond(start <= query_pos[-1], forward_work, lambda state: state, carry)

    start_state = (
        jnp.full((batch, HEADS, rows), START_MAX, jnp.float32),
        jnp.zeros((batch, HEADS, rows), jnp.float32),
        jnp.zeros((batch, HEADS, rows, HEAD_DIM), jnp.float32),
    )
    final_max, final_sum, accum = over_blocks(
        start_state,
        (
            lax.all_gather(key_rows, "sq", axis=1, tiled=True),
            lax.all_gather(value_rows, "sq", axis=1, tiled=True),
        ),
        jnp.int32(0),
        forward_step,
        512,
    )
    attended = heads_flat(accum / final_sum[..., None], batch, rows, width)
    log_total = final_max + jnp.log(final_sum)
    attended_low = attended.astype(jnp.bfloat16)
    middle = frames_own + jnp.dot(attended_low, w_out, preferred_element_type=jnp.float32)
    hidden2, norm2_pull = jax.vjp(norm_scaled, middle, norm2_gain)
    hidden2_low = hidden2.astype(jnp.bfloat16)
    upward = jnp.dot(hidden2_low, w_up, preferred_element_type=jnp.float32)
    active, gelu_pull = jax.vjp(jax.nn.gelu, upward)
    active_low = active.astype(jnp.bfloat16)
    result = middle + jnp.dot(active_low, w_down, preferred_element_type=jnp.float32)
    grad_top = cotangent.reshape(batch * rows, width).astype(jnp.float32)
    grad_branch = grad_top.astype(jnp.bfloat16)
    grad_down = contract_rows(active_low, grad_branch)
    grad_active = times_transpose(grad_branch, w_down)
    grad_upward = gelu_pull(grad_active)[0].astype(jnp.bfloat16)
    grad_up = contract_rows(hidden2_low, grad_upward)
    grad_hidden2 = times_transpose(grad_upward, w_up)
    grad_middle_part, grad_gain2 = norm2_pull(grad_hidden2)
    grad_middle = grad_top + grad_middle_part
    grad_attn = grad_middle.astype(jnp.bfloat16)
    grad_outproj = contract_rows(attended_low, grad_attn)
    grad_attended = times_transpose(grad_attn, w_out).astype(jnp.bfloat16)
    grad_rows_own = grad_attended.reshape(batch, rows, width)
    grad_heads = grad_attended.reshape(batch, rows, HEADS, HEAD_DIM)
    delta_rows = jnp.sum(
        (grad_attended.astype(jnp.float32) * attended).reshape(batch, rows, HEADS, HEAD_DIM), axis=3
    )
    delta = delta_rows.transpose(0, 2, 1)

    def query_step(carry, pieces, start):
        key_piece, value_piece = pieces
        count = key_piece.shape[1]
        key_pos = start + jnp.arange(count, dtype=jnp.int32)
        key_seg = segment_ids(key_pos, item_ends)

        def query_work(grad_query):
            keys_block = key_piece.reshape(batch, count, HEADS, HEAD_DIM)
            values_block = value_piece.reshape(batch, count, HEADS, HEAD_DIM)
            scores = (
                jnp.einsum(
                    "rqhd,rkhd->rhqk", queries, keys_block, preferred_element_type=jnp.float32
                )
                * factor
            )
            mask = visible(query_pos, query_seg, key_pos, key_seg)[:, None]
            shares = jnp.where(mask, jnp.exp(scores - log_total[..., None]), 0.0)
            grad_shares = jnp.einsum(
                "rqhd,rkhd->rhqk", grad_heads, values_block, preferred_element_type=jnp.float32
            )
            grad_scores = (shares * (grad_shares - delta[..., None])).astype(jnp.bfloat16)
            return grad_query + jnp.einsum(
                "rhqk,rkhd->rhqd", grad_scores, keys_block, preferred_element_type=jnp.float32
            )

        return lax.cond(start <= query_pos[-1], query_work, lambda state: state, carry)

    zero_query = jnp.zeros((batch, HEADS, rows, HEAD_DIM), jnp.float32)
    grad_query = over_blocks(
        zero_query,
        (
            lax.all_gather(key_rows, "sq", axis=1, tiled=True),
            lax.all_gather(value_rows, "sq", axis=1, tiled=True),
        ),
        jnp.int32(0),
        query_step,
        512,
    )

    def key_step(carry, pieces, start):
        query_piece, grad_piece, total_piece, delta_piece = pieces
        count = query_piece.shape[1]
        remote_pos = start + jnp.arange(count, dtype=jnp.int32)
        remote_seg = segment_ids(remote_pos, item_ends)

        def key_work(state):
            grad_key, grad_value = state
            remote_queries = query_piece.reshape(batch, count, HEADS, HEAD_DIM)
            remote_grads = grad_piece.reshape(batch, count, HEADS, HEAD_DIM)
            scores = (
                jnp.einsum(
                    "rqhd,rkhd->rhqk", remote_queries, keys_own, preferred_element_type=jnp.float32
                )
                * factor
            )
            mask = visible(remote_pos, remote_seg, query_pos, query_seg)[:, None]
            shares = jnp.where(
                mask, jnp.exp(scores - total_piece.transpose(0, 2, 1)[..., None]), 0.0
            )
            grad_value = grad_value + jnp.einsum(
                "rhqk,rqhd->rhkd",
                shares.astype(jnp.bfloat16),
                remote_grads,
                preferred_element_type=jnp.float32,
            )
            grad_shares = jnp.einsum(
                "rqhd,rkhd->rhqk", remote_grads, values_own, preferred_element_type=jnp.float32
            )
            grad_scores = (
                shares * (grad_shares - delta_piece.transpose(0, 2, 1)[..., None])
            ).astype(jnp.bfloat16)
            grad_key = grad_key + jnp.einsum(
                "rhqk,rqhd->rhkd", grad_scores, remote_queries, preferred_element_type=jnp.float32
            )
            return (grad_key, grad_value)

        return lax.cond(start + count - 1 >= first, key_work, lambda state: state, carry)

    grad_key, grad_value = over_blocks(
        (zero_query, zero_query),
        (
            lax.all_gather(query_rows, "sq", axis=1, tiled=True),
            lax.all_gather(grad_rows_own, "sq", axis=1, tiled=True),
            lax.all_gather(
                log_total.transpose(0, 2, 1).astype(jnp.bfloat16), "sq", axis=1, tiled=True
            ).astype(jnp.float32),
            lax.all_gather(delta_rows.astype(jnp.bfloat16), "sq", axis=1, tiled=True).astype(
                jnp.float32
            ),
        ),
        jnp.int32(0),
        key_step,
        512,
    )
    grad_mixed = jnp.concatenate(
        [
            heads_flat(grad_query * factor, batch, rows, width),
            heads_flat(grad_key * factor, batch, rows, width),
            heads_flat(grad_value, batch, rows, width),
        ],
        axis=1,
    ).astype(jnp.bfloat16)
    grad_qkv = contract_rows(hidden1_low, grad_mixed)
    grad_hidden1 = times_transpose(grad_mixed, w_qkv)
    grad_frames_part, grad_gain1 = norm1_pull(grad_hidden1)
    grad_frames = (grad_middle + grad_frames_part).reshape(batch, rows, width)
    result_rows = result.astype(jnp.bfloat16).reshape(batch, rows, width)
    shares_sq = (
        lax.psum_scatter(grad_gain1, "sq", scatter_dimension=0, tiled=True),
        lax.psum_scatter(grad_qkv, "sq", scatter_dimension=0, tiled=True),
        lax.psum_scatter(grad_outproj, "sq", scatter_dimension=0, tiled=True),
        lax.psum_scatter(grad_gain2, "sq", scatter_dimension=0, tiled=True),
        lax.psum_scatter(grad_up, "sq", scatter_dimension=0, tiled=True),
        lax.psum_scatter(grad_down, "sq", scatter_dimension=0, tiled=True),
    )
    totals = (
        lax.psum(shares_sq[0].astype(jnp.bfloat16), "dp").astype(jnp.float32),
        lax.psum(shares_sq[1].astype(jnp.bfloat16), "dp").astype(jnp.float32),
        lax.psum(shares_sq[2].astype(jnp.bfloat16), "dp").astype(jnp.float32),
        lax.psum(shares_sq[3].astype(jnp.bfloat16), "dp").astype(jnp.float32),
        lax.psum(shares_sq[4].astype(jnp.bfloat16), "dp").astype(jnp.float32),
        lax.psum(shares_sq[5].astype(jnp.bfloat16), "dp").astype(jnp.float32),
    )
    return (
        result_rows,
        grad_frames,
        totals[0],
        totals[1],
        totals[2],
        totals[3],
        totals[4],
        totals[5],
    )


def solution(mesh):
    return jax.shard_map(
        shards,
        mesh=mesh,
        in_specs=(
            P("dp", "sq", None),
            P(),
            P(),
            P(),
            P(),
            P(),
            P(),
            P("dp", None),
            P("dp", "sq", None),
        ),
        out_specs=(
            P("dp", "sq", None),
            P("dp", "sq", None),
            P("sq"),
            P("sq", None),
            P("sq", None),
            P("sq"),
            P("sq", None),
            P("sq", None),
        ),
        check_vma=False,
    )
```

profile of v0, /device:TPU:0, one launch (start us, length us, event | category | flops | bytes accessed | tf_op | source)
XLA Modules:
  0.0 698.9 jit_solution(101815978232163255)
XLA Ops:
  18.7 26.0 %all-gather.9.cloned.1.call-done = bf16[1024,1024]{1,0:T(8,128)(2,1)} async-done(((bf16[128,1024]{1,0:T(8,128)(2,1)}), bf16[1024,1024]{1,0:T(8,128)(2,1)}) %all-gather.9.cloned.1.call-update) | async-done | bytes 2097168 | tf_op jit(solution)/shard_map/all_gather | solution.py:131
  48.6 26.5 %all-gather.11.cloned.1.call-done = bf16[1024,1024]{1,0:T(8,128)(2,1)} async-done(((bf16[128,1024]{1,0:T(8,128)(2,1)}), bf16[1024,1024]{1,0:T(8,128)(2,1)}) %all-gather.11.cloned.1.call-update) | async-done | bytes 2097168 | tf_op jit(solution)/shard_map/all_gather | solution.py:132
  79.1 13.9 %while.45 = (s32[]{:T(128)}, f32[1,16,128]{2,1,0:T(8,128)S(1)}, f32[1,16,128]{2,1,0:T(8,128)S(1)}, f32[1,16,128,64]{2,3,1,0:T(8,128)S(1)}, s32[2]{0:T(128)S(1)},...) while((s32[]{:T(128)}, f32[1,16,128]{2,1,0:T(8,128)S(1)}, ...), condition=%wide.region_9.10_spmd, body=%wide.region_3.9_spmd.sunk | while | flops 282544640 | bytes 20628860 | solution.py:52
  83.0 6.1 conditional.8
  103.2 7.7 %fusion.60 = bf16[128,4096]{1,0:T(8,128)(2,1)S(1)} fusion(f32[128,4096]{1,0:T(8,128)S(1)} %fusion.92, bf16[4096,1024]{1,0:T(8,128)(2,1)} %param.27, bf16[1,128,1024]{2,1,0:T(8,128)(2,1)S(1)} %copy-done.18), kind=kOutput, calls=%fused_computation.80 | convolution fusion | flops 1084227584 | bytes 11796480 | tf_op jit(solution)/shard_map/dot_general | solution.py:62
  129.7 15.0 %all_gather.25 = bf16[1,1024,16]{1,2,0:T(8,128)(2,1)S(1)} all-gather(bf16[1,128,16]{1,2,0:T(8,128)(2,1)S(1)} %bitcast_convert_fusion), channel_id=1, replica_groups=mesh['dp'=4,'sq'=8] {'sq'}, dimensions={1}, use_global_device_ids=true | all-gather | bytes 36864 | tf_op jit(solution)/shard_map/all_gather | solution.py:253
  145.3 8.0 %all_gather.23 = bf16[1,1024,16]{1,2,0:T(8,128)(2,1)S(1)} all-gather(bf16[1,128,16]{1,2,0:T(8,128)(2,1)S(1)} %get-tuple-element.1073), channel_id=1, replica_groups=mesh['dp'=4,'sq'=8] {'sq'}, dimensions={1}, use_global_device_ids=true | all-gather | bytes 36864 | tf_op jit(solution)/shard_map/all_gather | solution.py:250
  155.3 20.4 %while.46 = (s32[]{:T(128)}, f32[1,16,128,64]{2,3,1,0:T(8,128)}, s32[2]{0:T(128)}, s32[128]{0:T(128)}, s32[1,8]{1,0:T(1,128)}, /*index=5*/s32[1,128]{1,0:T(1,128...) while((s32[]{:T(128)}, f32[1,16,128,64]{2,3,1,0:T(8,128)}, ...), condition=%wide.region_17.18_spmd, body=%wide.region_13.17_spmd.sunk | while | flops 409285120 | bytes 17499484 | solution.py:52
  159.7 11.6 %conditional.9 = (f32[1,16,128,64]{2,3,1,0:T(8,128)}) conditional(s32[]{:T(128)} %convert_element_type.291, f32[1,16,128,64]{2,3,1,0:T(8,128)} %get-tuple-element.1437, (s32[]{:T(128)}, s32[512]{0:T(512)S(1)}, s32[128]{0:T(128)}, s32[1,512,8]{1,2,0:T(8,128)S(1)}, s32[1,128]{1,0:T(1,128)}, /*index=5*/bf16[2,1,512,1024]{2,3,1,0:T(8,128)(2,1)}, ...), branch_computations={%region_14.14_spmd, %region_15.16_spmd} | conditional | flops 409276416 | bytes 17476628 | solution.py:192
  182.4 36.2 %while.47 = (s32[]{:T(128)}, f32[1,16,128,64]{2,3,1,0:T(8,128)S(1)}, f32[1,16,128,64]{2,3,1,0:T(8,128)}, s32[2]{0:T(128)S(1)}, s32[]{:T(128)}, /*index=5*/s32[1,...) while((s32[]{:T(128)}, ...), condition=%wide.region_22.23_spmd.clone.clone, body=%wide.region_18.22_spmd.clone.clone.sunk | while | flops 547828352 | bytes 28265440 | solution.py:52
  184.5 16.3 %conditional.10 = ((f32[1,16,128,64]{2,3,1,0:T(8,128)S(1)}, f32[1,16,128,64]{2,3,1,0:T(8,128)})) conditional(s32[]{:T(128)} %convert_element_type.293, (f32[1,16,128,64]{2,3,1,0:T(8,128)S(1)}, f32[1,16,128,64]{2,3,1,0:T(8,128)}) %tuple.150, (s32[]{:T(128)}, s32[]{:T(128)}, s32[512]{0:T(512)S(1)}, s32[1,128]{1,0:T(1,128)S(1)}, ...), branch_computations={%region_19.19_spmd, %region_20.21_spmd} | conditional | flops 547819648 | bytes 28242020 | solution.py:243
  190.0 6.2 fusion.42
  202.8 15.9 %conditional.10 = ((f32[1,16,128,64]{2,3,1,0:T(8,128)S(1)}, f32[1,16,128,64]{2,3,1,0:T(8,128)})) conditional(s32[]{:T(128)} %convert_element_type.293, (f32[1,16,128,64]{2,3,1,0:T(8,128)S(1)}, f32[1,16,128,64]{2,3,1,0:T(8,128)}) %tuple.150, (s32[]{:T(128)}, s32[]{:T(128)}, s32[512]{0:T(512)S(1)}, s32[1,128]{1,0:T(1,128)S(1)}, ...), branch_computations={%region_19.19_spmd, %region_20.21_spmd} | conditional | flops 547819648 | bytes 28242020 | solution.py:243
  208.3 6.2 fusion.42
  219.8 7.5 %fusion.72 = f32[1024,3072]{1,0:T(8,128)} fusion(bf16[128,1024]{0,1:T(8,128)(2,1)S(1)} %bitcast.228, bf16[128,1024]{0,1:T(8,128)(2,1)S(1)} %bitcast.230, bf16[128,1024]{0,1:T(8,128)(2,1)} %bitcast.226, bf16[1,128,1024]{2,1,0:T(8,128)(2,1)S(1)} %copy-done.4, f32[1024]{0:T(1024)S(1)} %copy-done.30, f32[128]{0:T(128)S(1)} %copy-done.38), kind=kOutput, calls=%fused_computation.111 | convolution fusion | flops 808189952 | bytes 13636096 | tf_op jit(solution)/shard_map/dot_general | solution.py:56
  228.5 11.2 %fusion.91 = f32[1024,4096]{1,0:T(8,128)} fusion(bf16[128,4096]{1,0:T(8,128)(2,1)S(1)} %copy-done.9, f32[128,1024]{1,0:T(8,128)S(1)} %get-tuple-element.1089, f32[1024]{0:T(1024)S(1)} %copy-done.29, f32[128]{0:T(128)S(1)} %copy-done.35), kind=kOutput, calls=%fused_computation.140 | convolution fusion | flops 1074135040 | bytes 18354688 | tf_op jit(solution)/shard_map/dot_general | solution.py:56
  241.9 8.9 %fusion.74 = f32[4096,1024]{1,0:T(8,128)} fusion(bf16[1,128,1024]{2,1,0:T(8,128)(2,1)S(1)} %copy-done.19, f32[128,4096]{1,0:T(8,128)S(1)} %copy-done.3), kind=kOutput, calls=%fused_computation.113 | convolution fusion | flops 1078460416 | bytes 19136512 | tf_op jit(solution)/shard_map/dot_general | solution.py:56
  252.8 67.5 %reduce-scatter.5.cloned.1.call-done = f32[128,3072]{1,0:T(8,128)} async-done(((f32[1024,3072]{1,0:T(8,128)}), f32[128,3072]{1,0:T(8,128)}) %reduce-scatter.5.cloned.1.call-update) | async-done | bytes 1572880 | tf_op jit(solution)/shard_map/reduce_scatter | solution.py:276
  322.6 117.6 %reduce-scatter.9.cloned.1.call-done = f32[128,4096]{1,0:T(8,128)} async-done(((f32[1024,4096]{1,0:T(8,128)}), f32[128,4096]{1,0:T(8,128)}) %reduce-scatter.9.cloned.1.call-update) | async-done | bytes 2097168 | tf_op jit(solution)/shard_map/reduce_scatter | solution.py:279
  442.9 117.3 %reduce-scatter.11.cloned.1.call-done = f32[512,1024]{1,0:T(8,128)} async-done(((f32[4096,1024]{1,0:T(8,128)}), f32[512,1024]{1,0:T(8,128)}) %reduce-scatter.11.cloned.1.call-update) | async-done | bytes 2097168 | tf_op jit(solution)/shard_map/reduce_scatter | solution.py:280
  564.8 5.7 fusion.62
  575.8 13.8 %all-reduce.2 = (bf16[1024]{0:T(1024)(128)(2,1)S(1)}, bf16[1024]{0:T(1024)(128)(2,1)S(1)}) all-reduce(f32[1024]{0:T(1024)S(1)} %get-tuple-element.989, f32[1024]{0:T(1024)S(1)} %copy-done.36), channel_id=6, replica_groups=mesh['dp'=4,'sq'=8] {'sq'}, use_global_device_ids=true, to_apply=%region_25.26.clone | all-reduce | flops 2048 | bytes 12288
  589.8 12.4 %all-reduce.3 = (bf16[128]{0:T(256)(128)(2,1)S(1)}, bf16[128]{0:T(256)(128)(2,1)S(1)}) all-reduce(bf16[128]{0:T(256)(128)(2,1)S(1)} %dynamic-slice.7, bf16[128]{0:T(256)(128)(2,1)S(1)} %dynamic-slice.6), channel_id=1, replica_groups=mesh['dp'=4,'sq'=8] {'dp'}, use_global_device_ids=true, to_apply=%region_26.27 | all-reduce | flops 256 | bytes 1024 | tf_op jit(solution)/shard_map/psum | solution.py:283
  604.2 81.7 %all-reduce.7.cloned.1.call-done = (bf16[128,3072]{1,0:T(8,128)(2,1)}, bf16[128,1024]{1,0:T(8,128)(2,1)}, bf16[128,4096]{1,0:T(8,128)(2,1)}, bf16[512,1024]{1,0:T(8,128)(2,1)}) async-done(((bf16[128,3072]{1,0:T(8,128)(2,1)}, bf16[128,1024]{1,0:T(8,128)(2,1)}, bf16[128,4096]{1,0:T(8,128)(2,1)}, bf16[512,1024]{1,0:T(8,128)(2,1)}), (bf16[128,3072]{1,0:T(8,128)(2,1)}, bf16[128,1024]{1,0:T(8,128)(2,1)}, ...) | async-done | bytes 3145744 | tf_op jit(solution)/shard_map/psum | solution.py:284
  (242 shorter events, 138.3 us)
Async XLA Ops:
  7.2 89.5 %copy-start = (bf16[1024,1024]{1,0:T(8,128)(2,1)S(1)}, bf16[1024,1024]{1,0:T(8,128)(2,1)}, u32[]{:S(2)}) copy-start(bf16[1024,1024]{1,0:T(8,128)(2,1)} %param.24) | copy-start | bytes 6291460
  7.2 37.5 %all-gather.9.cloned.1.call-start = ((), (), s32[]{:S(2)}) async-start(), calls=%async_computation.8 | async-start | bytes 2359296 | tf_op jit(solution)/shard_map/all_gather | solution.py:131
  14.0 61.1 %all-gather.11.cloned.1.call-start = ((), (), s32[]{:S(2)}) async-start(), calls=%async_computation.9 | async-start | bytes 2359296 | tf_op jit(solution)/shard_map/all_gather | solution.py:132
  14.7 109.4 %all-gather.13.cloned.1.call-start = ((), (), s32[]{:S(2)}) async-start(), calls=%async_computation.10 | async-start | bytes 2359296 | tf_op jit(solution)/shard_map/all_gather | solution.py:248
  15.4 162.1 %all-gather.15.cloned.1.call-start = ((), (), s32[]{:S(2)}) async-start(), calls=%async_computation.11 | async-start | bytes 2359296 | tf_op jit(solution)/shard_map/all_gather | solution.py:249
  98.2 16.3 %copy-start.34 = (f32[128]{0:T(128)}, f32[128]{0:T(128)S(1)}, u32[]{:S(2)}) copy-start(f32[128]{0:T(128)S(1)} %fusion.88) | copy-start | bytes 1540
  98.3 12.7 %slice-start = ((s8[8388608]{0:T(1024)(128)(4,1)}), s8[4194304]{0:T(1024)(128)(4,1)S(1)}, s32[]{:S(2)}) async-start(s8[8388608]{0:T(1024)(128)(4,1)} %bitcast.209), calls=%async_computation.13 | async-start | bytes 8388608
  103.2 7.8 %copy-start.2 = (f32[128,4096]{1,0:T(8,128)}, f32[128,4096]{1,0:T(8,128)S(1)}, u32[]{:S(2)}) copy-start(f32[128,4096]{1,0:T(8,128)S(1)} %fusion.92) | copy-start | bytes 6291460
  103.2 7.8 %slice-start.1 = ((s8[8388608]{0:T(1024)(128)(4,1)}), s8[4194304]{0:T(1024)(128)(4,1)S(1)}, s32[]{:S(2)}) async-start(s8[8388608]{0:T(1024)(128)(4,1)} %bitcast.209), calls=%async_computation.14 | async-start | bytes 8388608
  117.3 133.6 %reduce-scatter.7.cloned.1.call-start = ((), (), s32[]{:S(2)}) async-start(), calls=%async_computation.5 | async-start | bytes 4718592 | tf_op jit(solution)/shard_map/reduce_scatter | solution.py:277
  121.3 198.9 %reduce-scatter.5.cloned.1.call-start = ((), (), s32[]{:S(2)}) async-start(), calls=%async_computation.4 | async-start | bytes 14155776 | tf_op jit(solution)/shard_map/reduce_scatter | solution.py:276
  182.4 37.4 %copy-start.30 = (f32[1024]{0:T(1024)S(1)}, f32[1024]{0:T(1024)}, u32[]{:S(2)}) copy-start(f32[1024]{0:T(1024)} %param.22) | copy-start | bytes 12292
  182.4 37.4 %copy-start.38 = (f32[128]{0:T(128)S(1)}, f32[128]{0:T(128)}, u32[]{:S(2)}) copy-start(f32[128]{0:T(128)} %copy-done.37) | copy-start | bytes 1540
  219.7 7.6 %copy-start.23 = (bf16[1,16,128,64]{2,3,1,0:T(8,128)(2,1)}, bf16[1,16,128,64]{2,3,1,0:T(8,128)(2,1)S(1)}, u32[]{:S(2)}) copy-start(bf16[1,16,128,64]{2,3,1,0:T(8,128)(2,1)S(1)} %convert.20) | copy-start | bytes 786436
  219.8 7.5 %copy-start.25 = (bf16[1,16,128,64]{2,3,1,0:T(8,128)(2,1)}, bf16[1,16,128,64]{2,3,1,0:T(8,128)(2,1)S(1)}, u32[]{:S(2)}) copy-start(bf16[1,16,128,64]{2,3,1,0:T(8,128)(2,1)S(1)} %multiply_convert_fusion.2) | copy-start | bytes 786436
  227.3 212.8 %reduce-scatter.9.cloned.1.call-start = ((), (), s32[]{:S(2)}) async-start(), calls=%async_computation.6 | async-start | bytes 18874368 | tf_op jit(solution)/shard_map/reduce_scatter | solution.py:279
  239.7 320.4 %reduce-scatter.11.cloned.1.call-start = ((), (), s32[]{:S(2)}) async-start(), calls=%async_computation.7 | async-start | bytes 18874368 | tf_op jit(solution)/shard_map/reduce_scatter | solution.py:280
  250.9 435.0 %all-reduce.7.cloned.1.call-start = ((), (), s32[]{:S(2)}) async-start(), calls=%async_computation.12 | async-start | bytes 6291456 | tf_op jit(solution)/shard_map/psum | solution.py:284
  564.8 5.8 copy-start.22
  564.8 5.8 copy-start.24
  564.8 5.8 copy-start.26
  564.8 5.8 copy-start.39
  570.6 32.6 %copy-start.41 = (f32[128]{0:T(128)S(1)}, f32[128]{0:T(128)}, u32[]{:S(2)}) copy-start(f32[128]{0:T(128)} %copy-done.40) | copy-start | bytes 1540
  570.6 32.6 %copy-start.6 = (f32[128,1024]{1,0:T(8,128)S(1)}, f32[128,1024]{1,0:T(8,128)}, u32[]{:S(2)}) copy-start(f32[128,1024]{1,0:T(8,128)} %copy-done.5) | copy-start | bytes 1572868
  (33 other events, 85.8 us)
Sparse Core Ops, SparseCore 0:
  14.1 30.5 all-gather.8
  47.2 27.8 all-gather.10
  77.0 27.8 all-gather.12
  117.5 34.1 all-gather.14
  154.8 51.3 reduce-scatter.6
  227.5 92.7 reduce-scatter.4
  324.2 115.9 reduce-scatter.8
  444.2 115.9 reduce-scatter.10
  563.5 122.3 all-reduce.6
where the time goes:
time: 700 us; the launch traced here: 699 us
  waiting for transfers between devices  438 us (63%)
  matrix products  103 us (15%)
  local copies, waits for them, and re-layouts  50.6 us (7%)
  blocking collectives  49.2 us (7%)
  other arithmetic  35.8 us (5%)
  between operations  15 us (2%)
    reduce_scatter x1, waiting for transfers between devices, shards(): lax.psum_scatter(grad_up, 'sq', scatter_dimension=0, tiled=True)  118 us
    reduce_scatter x1, waiting for transfers between devices, shards(): lax.psum_scatter(grad_down, 'sq', scatter_dimension=0, tiled=True)  117 us
    psum x1, waiting for transfers between devices, shards(): lax.psum(shares_sq[1].astype(jnp.bfloat16), 'dp').astype(jnp.float32)  81.7 us
    reduce_scatter x1, waiting for transfers between devices, shards(): lax.psum_scatter(grad_qkv, 'sq', scatter_dimension=0, tiled=True)  67.5 us
    dot_general x4, matrix products, contract_rows(): lax.dot_general(left, right, (((0,), (0,)), ((), ())), preferred_element_...  31.4 us
    all_gather x1, waiting for transfers between devices, shards(): lax.all_gather(value_rows, 'sq', axis=1, tiled=True)  26.5 us
    all_gather x1, waiting for transfers between devices, shards(): lax.all_gather(key_rows, 'sq', axis=1, tiled=True)  26 us
    dot_general x4, matrix products, times_transpose(): lax.dot_general(left, right, (((1,), (1,)), ((), ())), preferred_element_...  18.2 us
  transfers between devices with their start and end apart: 9, of which 6 were waited for; matrix products, arithmetic and copies ran while one was open for 24% of the time, Pallas kernels for 0%

commit v1 on v0

--- a/solution.py
+++ b/solution.py
@@ -8,6 +8,17 @@
 EPSILON = 1e-05
 NEG_FILL = -1000000000.0
 START_MAX = -1e30
+
+
+def ring_gather(x, axis, dim):
+    ways = lax.axis_size(axis)
+    pieces = [x]
+    for far in range(1, ways):
+        pieces.append(
+            lax.ppermute(pieces[far - 1], axis, [(d, (d - 1) % ways) for d in range(ways)])
+        )
+    line = jnp.concatenate(pieces, axis=dim)
+    return jnp.roll(line, lax.axis_index(axis) * x.shape[dim], axis=dim)
 
 
 def norm_scaled(values, gain):
@@ -127,10 +138,7 @@
     )
     final_max, final_sum, accum = over_blocks(
         start_state,
-        (
-            lax.all_gather(key_rows, "sq", axis=1, tiled=True),
-            lax.all_gather(value_rows, "sq", axis=1, tiled=True),
-        ),
+        (lax.all_gather(key_rows, "sq", axis=1, tiled=True), ring_gather(value_rows, "sq", 1)),
         jnp.int32(0),
         forward_step,
         512,

time: 700 us -> 714 us (1.020)
  waiting for transfers between devices: 438 us -> 410 us
  starting transfers between devices: 0.63 us -> 21 us
  local copies, waits for them, and re-layouts: 50.6 us -> 61.4 us
    all_gather x1, waiting for transfers between devices: 26.5 us -> 0.01 us  [shards(): lax.all_gather(value_rows, 'sq', axis=1, tiled=True)]
    all_gather x1, waiting for transfers between devices: 26 us -> 0.01 us  [shards(): lax.all_gather(key_rows, 'sq', axis=1, tiled=True)]
    ppermute x0 -> x7, waiting for transfers between devices: none -> 24.7 us  [ring_gather(): lax.ppermute(pieces[far - 1], axis, [(d, (d - 1) % ways) for d in range(w...]
    ppermute x0 -> x7, starting transfers between devices: none -> 20.4 us  [ring_gather(): lax.ppermute(pieces[far - 1], axis, [(d, (d - 1) % ways) for d in range(w...]
    unnamed x94 -> x109, local copies, waits for them, and re-layouts: 17.1 us -> 22.1 us
  transfers between devices with their start and end apart: 9 -> 16, of which waited for: 6 -> 11; matrix products, arithmetic and copies ran while one was open for 24% -> 25% of each run, Pallas kernels for 0% -> 0%
where the time goes in v1:
time: 714 us; the launch traced here: 707 us
  waiting for transfers between devices  410 us (57%)
  matrix products  103 us (14%)
  local copies, waits for them, and re-layouts  61.4 us (9%)
  blocking collectives  49.2 us (7%)
  other arithmetic  39.9 us (6%)
  starting transfers between devices  21 us (3%)
  between operations  15.4 us (2%)
    reduce_scatter x1, waiting for transfers between devices, shards(): lax.psum_scatter(grad_up, 'sq', scatter_dimension=0, tiled=True)  118 us
    reduce_scatter x1, waiting for transfers between devices, shards(): lax.psum_scatter(grad_down, 'sq', scatter_dimension=0, tiled=True)  117 us
    psum x1, waiting for transfers between devices, shards(): lax.psum(shares_sq[1].astype(jnp.bfloat16), 'dp').astype(jnp.float32)  82 us
    reduce_scatter x1, waiting for transfers between devices, shards(): lax.psum_scatter(grad_qkv, 'sq', scatter_dimension=0, tiled=True)  67.4 us
    dot_general x4, matrix products, contract_rows(): lax.dot_general(left, right, (((0,), (0,)), ((), ())), preferred_element_...  31.6 us
    ppermute x7, waiting for transfers between devices, ring_gather(): lax.ppermute(pieces[far - 1], axis, [(d, (d - 1) % ways) for d in range(w...  24.7 us
    unnamed x109, local copies, waits for them, and re-layouts  22.1 us
    ppermute x7, starting transfers between devices, ring_gather(): lax.ppermute(pieces[far - 1], axis, [(d, (d - 1) % ways) for d in range(w...  20.4 us
  transfers between devices with their start and end apart: 16, of which 11 were waited for; matrix products, arithmetic and copies ran while one was open for 25% of the time, Pallas kernels for 0%

profile of v1, /device:TPU:0, one launch (start us, length us, event | category | flops | bytes accessed | tf_op | source)
XLA Modules:
  0.0 706.7 jit_solution(10757730638805886928)
XLA Ops:
  24.8 5.5 collective-permute-done.1
  80.0 14.4 %while.45 = (s32[]{:T(128)}, f32[1,16,128]{2,1,0:T(8,128)S(1)}, f32[1,16,128]{2,1,0:T(8,128)S(1)}, f32[1,16,128,64]{2,3,1,0:T(8,128)S(1)}, s32[2]{0:T(128)S(1)},...) while((s32[]{:T(128)}, f32[1,16,128]{2,1,0:T(8,128)S(1)}, ...), condition=%wide.region_9.10_spmd, body=%wide.region_3.9_spmd.sunk | while | flops 282544640 | bytes 20628860 | solution.py:63
  83.9 6.1 conditional.8
  104.9 7.8 %fusion.60 = bf16[128,4096]{1,0:T(8,128)(2,1)S(1)} fusion(f32[128,4096]{1,0:T(8,128)S(1)} %fusion.92, bf16[4096,1024]{1,0:T(8,128)(2,1)} %param.27, bf16[1,128,1024]{2,1,0:T(8,128)(2,1)S(1)} %copy-done.18), kind=kOutput, calls=%fused_computation.80 | convolution fusion | flops 1084227584 | bytes 11796480 | tf_op jit(solution)/shard_map/dot_general | solution.py:73
  130.5 15.0 %all_gather.24 = bf16[1,1024,16]{1,2,0:T(8,128)(2,1)S(1)} all-gather(bf16[1,128,16]{1,2,0:T(8,128)(2,1)S(1)} %bitcast_convert_fusion), channel_id=1, replica_groups=mesh['dp'=4,'sq'=8] {'sq'}, dimensions={1}, use_global_device_ids=true | all-gather | bytes 36864 | tf_op jit(solution)/shard_map/all_gather | solution.py:261
  146.1 7.7 %all_gather.22 = bf16[1,1024,16]{1,2,0:T(8,128)(2,1)S(1)} all-gather(bf16[1,128,16]{1,2,0:T(8,128)(2,1)S(1)} %get-tuple-element.1073), channel_id=1, replica_groups=mesh['dp'=4,'sq'=8] {'sq'}, dimensions={1}, use_global_device_ids=true | all-gather | bytes 36864 | tf_op jit(solution)/shard_map/all_gather | solution.py:258
  160.0 20.2 %while.46 = (s32[]{:T(128)}, f32[1,16,128,64]{2,3,1,0:T(8,128)}, s32[2]{0:T(128)}, s32[128]{0:T(128)}, s32[1,8]{1,0:T(1,128)}, /*index=5*/s32[1,128]{1,0:T(1,128...) while((s32[]{:T(128)}, f32[1,16,128,64]{2,3,1,0:T(8,128)}, ...), condition=%wide.region_17.18_spmd, body=%wide.region_13.17_spmd.sunk | while | flops 409285120 | bytes 17499484 | solution.py:63
  164.4 11.4 %conditional.9 = (f32[1,16,128,64]{2,3,1,0:T(8,128)}) conditional(s32[]{:T(128)} %convert_element_type.291, f32[1,16,128,64]{2,3,1,0:T(8,128)} %get-tuple-element.1438, (s32[]{:T(128)}, s32[512]{0:T(512)S(1)}, s32[128]{0:T(128)}, s32[1,512,8]{1,2,0:T(8,128)S(1)}, s32[1,128]{1,0:T(1,128)}, /*index=5*/bf16[2,1,512,1024]{2,3,1,0:T(8,128)(2,1)}, ...), branch_computations={%region_14.14_spmd, %region_15.16_spmd} | conditional | flops 409276416 | bytes 17476628 | solution.py:200
  170.6 5.2 fusion.23
  186.9 37.1 %while.47 = (s32[]{:T(128)}, f32[1,16,128,64]{2,3,1,0:T(8,128)S(1)}, f32[1,16,128,64]{2,3,1,0:T(8,128)}, s32[2]{0:T(128)S(1)}, s32[]{:T(128)}, /*index=5*/s32[1,...) while((s32[]{:T(128)}, ...), condition=%wide.region_22.23_spmd.clone.clone, body=%wide.region_18.22_spmd.clone.clone.sunk | while | flops 547828352 | bytes 28265440 | solution.py:63
  188.9 16.6 %conditional.10 = ((f32[1,16,128,64]{2,3,1,0:T(8,128)S(1)}, f32[1,16,128,64]{2,3,1,0:T(8,128)})) conditional(s32[]{:T(128)} %convert_element_type.293, (f32[1,16,128,64]{2,3,1,0:T(8,128)S(1)}, f32[1,16,128,64]{2,3,1,0:T(8,128)}) %tuple.151, (s32[]{:T(128)}, s32[]{:T(128)}, s32[512]{0:T(512)S(1)}, s32[1,128]{1,0:T(1,128)}, ...), branch_computations={%region_19.19_spmd, %region_20.21_spmd} | conditional | flops 547819648 | bytes 28242020 | solution.py:251
  195.1 6.2 fusion.42
  207.4 16.6 %conditional.10 = ((f32[1,16,128,64]{2,3,1,0:T(8,128)S(1)}, f32[1,16,128,64]{2,3,1,0:T(8,128)})) conditional(s32[]{:T(128)} %convert_element_type.293, (f32[1,16,128,64]{2,3,1,0:T(8,128)S(1)}, f32[1,16,128,64]{2,3,1,0:T(8,128)}) %tuple.151, (s32[]{:T(128)}, s32[]{:T(128)}, s32[512]{0:T(512)S(1)}, s32[1,128]{1,0:T(1,128)}, ...), branch_computations={%region_19.19_spmd, %region_20.21_spmd} | conditional | flops 547819648 | bytes 28242020 | solution.py:251
  213.6 6.2 fusion.42
  225.2 7.5 %fusion.72 = f32[1024,3072]{1,0:T(8,128)} fusion(bf16[128,1024]{0,1:T(8,128)(2,1)S(1)} %bitcast.234, bf16[128,1024]{0,1:T(8,128)(2,1)S(1)} %bitcast.236, bf16[128,1024]{0,1:T(8,128)(2,1)} %bitcast.232, bf16[1,128,1024]{2,1,0:T(8,128)(2,1)S(1)} %copy-done.4, f32[1024]{0:T(1024)S(1)} %copy-done.33, f32[128]{0:T(128)S(1)} %copy-done.38), kind=kOutput, calls=%fused_computation.111 | convolution fusion | flops 808189952 | bytes 13636096 | tf_op jit(solution)/shard_map/dot_general | solution.py:67
  233.9 11.3 %fusion.91 = f32[1024,4096]{1,0:T(8,128)} fusion(bf16[128,4096]{1,0:T(8,128)(2,1)S(1)} %copy-done.9, f32[128,1024]{1,0:T(8,128)S(1)} %get-tuple-element.1090, f32[1024]{0:T(1024)S(1)} %copy-done.32, f32[128]{0:T(128)S(1)} %copy-done.35), kind=kOutput, calls=%fused_computation.157 | convolution fusion | flops 1074135040 | bytes 18354688 | tf_op jit(solution)/shard_map/dot_general | solution.py:67
  247.4 8.9 %fusion.74 = f32[4096,1024]{1,0:T(8,128)} fusion(bf16[1,128,1024]{2,1,0:T(8,128)(2,1)S(1)} %copy-done.19, f32[128,4096]{1,0:T(8,128)S(1)} %copy-done.3), kind=kOutput, calls=%fused_computation.113 | convolution fusion | flops 1078460416 | bytes 19136512 | tf_op jit(solution)/shard_map/dot_general | solution.py:67
  258.1 67.4 %reduce-scatter.5.cloned.1.call-done = f32[128,3072]{1,0:T(8,128)} async-done(((f32[1024,3072]{1,0:T(8,128)}), f32[128,3072]{1,0:T(8,128)}) %reduce-scatter.5.cloned.1.call-update) | async-done | bytes 1572880 | tf_op jit(solution)/shard_map/reduce_scatter | solution.py:284
  327.9 117.6 %reduce-scatter.9.cloned.1.call-done = f32[128,4096]{1,0:T(8,128)} async-done(((f32[1024,4096]{1,0:T(8,128)}), f32[128,4096]{1,0:T(8,128)}) %reduce-scatter.9.cloned.1.call-update) | async-done | bytes 2097168 | tf_op jit(solution)/shard_map/reduce_scatter | solution.py:287
  448.2 117.3 %reduce-scatter.11.cloned.1.call-done = f32[512,1024]{1,0:T(8,128)} async-done(((f32[4096,1024]{1,0:T(8,128)}), f32[512,1024]{1,0:T(8,128)}) %reduce-scatter.11.cloned.1.call-update) | async-done | bytes 2097168 | tf_op jit(solution)/shard_map/reduce_scatter | solution.py:288
  569.5 5.7 fusion.62
  580.4 14.1 %all-reduce.2 = (bf16[1024]{0:T(1024)(128)(2,1)S(1)}, bf16[1024]{0:T(1024)(128)(2,1)S(1)}) all-reduce(f32[1024]{0:T(1024)S(1)} %get-tuple-element.989, f32[1024]{0:T(1024)S(1)} %copy-done.36), channel_id=6, replica_groups=mesh['dp'=4,'sq'=8] {'sq'}, use_global_device_ids=true, to_apply=%region_25.26.clone | all-reduce | flops 2048 | bytes 12288
  594.7 12.4 %all-reduce.3 = (bf16[128]{0:T(256)(128)(2,1)S(1)}, bf16[128]{0:T(256)(128)(2,1)S(1)}) all-reduce(bf16[128]{0:T(256)(128)(2,1)S(1)} %dynamic-slice.7, bf16[128]{0:T(256)(128)(2,1)S(1)} %dynamic-slice.6), channel_id=1, replica_groups=mesh['dp'=4,'sq'=8] {'dp'}, use_global_device_ids=true, to_apply=%region_26.27 | all-reduce | flops 256 | bytes 1024 | tf_op jit(solution)/shard_map/psum | solution.py:291
  609.2 82.0 %all-reduce.7.cloned.1.call-done = (bf16[128,3072]{1,0:T(8,128)(2,1)}, bf16[128,1024]{1,0:T(8,128)(2,1)}, bf16[128,4096]{1,0:T(8,128)(2,1)}, bf16[512,1024]{1,0:T(8,128)(2,1)}) async-done(((bf16[128,3072]{1,0:T(8,128)(2,1)}, bf16[128,1024]{1,0:T(8,128)(2,1)}, bf16[128,4096]{1,0:T(8,128)(2,1)}, bf16[512,1024]{1,0:T(8,128)(2,1)}), (bf16[128,3072]{1,0:T(8,128)(2,1)}, bf16[128,1024]{1,0:T(8,128)(2,1)}, ...) | async-done | bytes 3145744 | tf_op jit(solution)/shard_map/psum | solution.py:292
  (274 shorter events, 186.5 us)
Async XLA Ops:
  7.2 90.9 %copy-start = (bf16[1024,1024]{1,0:T(8,128)(2,1)S(1)}, bf16[1024,1024]{1,0:T(8,128)(2,1)}, u32[]{:S(2)}) copy-start(bf16[1024,1024]{1,0:T(8,128)(2,1)} %param.24) | copy-start | bytes 6291460
  7.2 68.8 %all-gather.9.cloned.1.call-start = ((), (), s32[]{:S(2)}) async-start(), calls=%async_computation.8 | async-start | bytes 2359296 | tf_op jit(solution)/shard_map/all_gather | solution.py:141
  9.0 31.6 %copy-start.42 = (s32[1,8]{1,0:T(1,128)S(1)}, s32[1,8]{1,0:T(1,128)}, u32[]{:S(2)}) copy-start(s32[1,8]{1,0:T(1,128)} %param.28) | copy-start | bytes 100
  13.9 111.1 %all-gather.13.cloned.1.call-start = ((), (), s32[]{:S(2)}) async-start(), calls=%async_computation.10 | async-start | bytes 2359296 | tf_op jit(solution)/shard_map/all_gather | solution.py:256
  14.7 139.2 %all-gather.11.cloned.1.call-start = ((), (), s32[]{:S(2)}) async-start(), calls=%async_computation.9 | async-start | bytes 2359296 | tf_op jit(solution)/shard_map/all_gather | solution.py:207
  14.7 7.3 %collective-permute-start = (bf16[1,128,1024]{2,1,0:T(8,128)(2,1)S(1)}, bf16[1,128,1024]{2,1,0:T(8,128)(2,1)S(1)}, u32[]{:S(2)}, u32[]{:S(2)}) collective-permute-start(bf16[1,128,1024]{2,1,0:T(8,128)(2,1)S(1)} %get-tuple-element.1086), channel_id=1, source_target_pairs={{0,7},{1,0},{2,1},{3,2},{4,3},{5,4},{6,5},{7,6},{8,15},{9,8},{10,9... | collective-permute-start | bytes 786440 | tf_op jit(solution)/shard_map/ppermute | solution.py:18
  22.0 8.3 %collective-permute-start.1 = (bf16[1,128,1024]{2,1,0:T(8,128)(2,1)S(1)}, bf16[1,128,1024]{2,1,0:T(8,128)(2,1)S(1)}, u32[]{:S(2)}, u32[]{:S(2)}) collective-permute-start(bf16[1,128,1024]{2,1,0:T(8,128)(2,1)S(1)} %collective-permute-done), channel_id=1, source_target_pairs={{0,7},{1,0},{2,1},{3,2},{4,3},{5,4},{6,5},{7,6},{8,15},{9,8},{10,9... | collective-permute-start | bytes 786440 | tf_op jit(solution)/shard_map/ppermute | solution.py:18
  31.0 6.8 collective-permute-start.2
  37.8 8.8 %collective-permute-start.3 = (bf16[1,128,1024]{2,1,0:T(8,128)(2,1)S(1)}, bf16[1,128,1024]{2,1,0:T(8,128)(2,1)}, u32[]{:S(2)}, u32[]{:S(2)}) collective-permute-start(bf16[1,128,1024]{2,1,0:T(8,128)(2,1)S(1)} %collective-permute-done.2), channel_id=1, source_target_pairs={{0,7},{1,0},{2,1},{3,2},{4,3},{5,4},{6,5},{7,6},{8,15},{9,8},{10,9... | collective-permute-start | bytes 786440 | tf_op jit(solution)/shard_map/ppermute | solution.py:18
  40.6 141.5 %all-gather.15.cloned.1.call-start = ((), (), s32[]{:S(2)}) async-start(), calls=%async_computation.11 | async-start | bytes 2359296 | tf_op jit(solution)/shard_map/all_gather | solution.py:257
  46.5 7.2 %collective-permute-start.4 = (bf16[1,128,1024]{2,1,0:T(8,128)(2,1)}, bf16[1,128,1024]{2,1,0:T(8,128)(2,1)}, u32[]{:S(2)}, u32[]{:S(2)}) collective-permute-start(bf16[1,128,1024]{2,1,0:T(8,128)(2,1)} %collective-permute-done.3), channel_id=1, source_target_pairs={{0,7},{1,0},{2,1},{3,2},{4,3},{5,4},{6,5},{7,6},{8,15},{9,8},{10,9... | collective-permute-start | bytes 786440 | tf_op jit(solution)/shard_map/ppermute | solution.py:18
  53.7 8.0 %collective-permute-start.5 = (bf16[1,128,1024]{2,1,0:T(8,128)(2,1)}, bf16[1,128,1024]{2,1,0:T(8,128)(2,1)S(1)}, u32[]{:S(2)}, u32[]{:S(2)}) collective-permute-start(bf16[1,128,1024]{2,1,0:T(8,128)(2,1)} %collective-permute-done.4), channel_id=1, source_target_pairs={{0,7},{1,0},{2,1},{3,2},{4,3},{5,4},{6,5},{7,6},{8,15},{9,8},{10,9... | collective-permute-start | bytes 786440 | tf_op jit(solution)/shard_map/ppermute | solution.py:18
  61.7 6.6 collective-permute-start.6
  80.0 18.1 %copy-start.4 = (bf16[1,128,1024]{2,1,0:T(8,128)(2,1)S(1)}, bf16[1,128,1024]{2,1,0:T(8,128)(2,1)}, u32[]{:S(2)}) copy-start(bf16[1,128,1024]{2,1,0:T(8,128)(2,1)} %param.21) | copy-start | bytes 786436
  119.1 137.2 %reduce-scatter.7.cloned.1.call-start = ((), (), s32[]{:S(2)}) async-start(), calls=%async_computation.5 | async-start | bytes 4718592 | tf_op jit(solution)/shard_map/reduce_scatter | solution.py:285
  123.1 202.4 %reduce-scatter.5.cloned.1.call-start = ((), (), s32[]{:S(2)}) async-start(), calls=%async_computation.4 | async-start | bytes 14155776 | tf_op jit(solution)/shard_map/reduce_scatter | solution.py:284
  186.9 38.3 %copy-start.33 = (f32[1024]{0:T(1024)S(1)}, f32[1024]{0:T(1024)}, u32[]{:S(2)}) copy-start(f32[1024]{0:T(1024)} %param.22) | copy-start | bytes 12292
  186.9 38.3 %copy-start.38 = (f32[128]{0:T(128)S(1)}, f32[128]{0:T(128)}, u32[]{:S(2)}) copy-start(f32[128]{0:T(128)} %copy-done.37) | copy-start | bytes 1540
  232.7 212.7 %reduce-scatter.9.cloned.1.call-start = ((), (), s32[]{:S(2)}) async-start(), calls=%async_computation.6 | async-start | bytes 18874368 | tf_op jit(solution)/shard_map/reduce_scatter | solution.py:287
  245.2 320.2 %reduce-scatter.11.cloned.1.call-start = ((), (), s32[]{:S(2)}) async-start(), calls=%async_computation.7 | async-start | bytes 18874368 | tf_op jit(solution)/shard_map/reduce_scatter | solution.py:288
  256.3 435.0 %all-reduce.7.cloned.1.call-start = ((), (), s32[]{:S(2)}) async-start(), calls=%async_computation.12 | async-start | bytes 6291456 | tf_op jit(solution)/shard_map/psum | solution.py:292
  327.9 240.3 %copy-start.43 = (u32[32]{0:T(128)S(1)}, u32[32]{0:T(128)}, u32[]{:S(2)}) copy-start(u32[32]{0:T(128)} %constant.187) | copy-start | bytes 388
  575.2 33.0 %copy-start.41 = (f32[128]{0:T(128)S(1)}, f32[128]{0:T(128)}, u32[]{:S(2)}) copy-start(f32[128]{0:T(128)} %copy-done.40) | copy-start | bytes 1540
  575.2 33.0 %copy-start.6 = (f32[128,1024]{1,0:T(8,128)S(1)}, f32[128,1024]{1,0:T(8,128)}, u32[]{:S(2)}) copy-start(f32[128,1024]{1,0:T(8,128)} %copy-done.5) | copy-start | bytes 1572868
  (40 other events, 220.8 us)
Sparse Core Ops, SparseCore 0:
  14.0 35.5 all-gather.8
  51.5 28.9 all-gather.12
  82.9 27.8 all-gather.10
  119.2 35.2 all-gather.14
  157.7 51.3 reduce-scatter.6
  232.8 92.6 reduce-scatter.4
  329.5 115.9 reduce-scatter.8
  449.4 115.9 reduce-scatter.10
  568.8 122.3 all-reduce.6
